TPU v7x, 32 devices: a whole 2x2x4 slice. The times are simulated.
32 devices in a mesh: ha: 8 (over y, x, core), wa: 4 (over z).
Axes of the slice: x: 2, y: 2, z: 4, core: 2. Of those that a mesh axis runs over, the one named last changes fastest.
Arguments:
- tokens: bfloat16 [128, 64, 256], P('ha', 'wa'), may hold values from -6 to 6
- gain_attn: float32 [256], replicated, may hold values from 0.25 to 1.75
- qkv_fine: bfloat16 [256, 768], replicated, may hold values from -0.375 to 0.375
- scale_fine: float32 [4], replicated, may hold values from 2 to 24
- out_fine: bfloat16 [256, 256], replicated, may hold values from -0.375 to 0.375
- gain_ffn: float32 [256], replicated, may hold values from 0.25 to 1.75
- ffn_in: bfloat16 [256, 1536], replicated, may hold values from -0.375 to 0.375
- ffn_out: bfloat16 [768, 256], replicated, may hold values from -0.21875 to 0.21875
- up_proj: bfloat16 [256, 1024], replicated, may hold values from -0.375 to 0.375
- gain_coarse: float32 [1024], replicated, may hold values from 0.25 to 1.75
- qkv_coarse: bfloat16 [1024, 3072], replicated, may hold values from -0.1875 to 0.1875
- scale_coarse: float32 [16], replicated, may hold values from 2 to 24
- out_coarse: bfloat16 [1024, 1024], replicated, may hold values from -0.1875 to 0.1875
Outputs:
- fine_out: bfloat16 [128, 64, 256], P('ha', 'wa')
- coarse_out: bfloat16 [8, 4, 1024], P('ha', 'wa')
All inputs are finite; a program needn't handle non-finite values.
Results may differ from a plain program's by a relative error of at most 0.03.
Values may be sent and summed in bfloat16 or wider, within the bound.
No kernel may reach another device: no remote copies, remote signals or barrier semaphores. Data moves between devices by JAX's collectives and lax.ppermute only.
A program may use at most 128 MiB of HBM per device.

v0:
```python
import jax
import jax.numpy as jnp
from jax import lax
from jax.sharding import PartitionSpec as P

CC = 1024
HD = 64
FFH = 768
RADIUS = 3
POOL = 16


def with_halo(cells, sides, width):
    for axis, dim in sides:
        count = lax.axis_size(axis)
        ends = count - 1
        head = lax.slice_in_dim(cells, 0, width, axis=dim)
        tail = lax.slice_in_dim(cells, cells.shape[dim] - width, cells.shape[dim], axis=dim)
        cells = jnp.concatenate(
            [
                lax.ppermute(tail, axis, [(i, (i + 1) % count) for i in range(ends)]),
                cells,
                lax.ppermute(head, axis, [((i + 1) % count, i) for i in range(ends)]),
            ],
            axis=dim,
        )
    return cells


def rms_scale(values, gain):
    values = values.astype(jnp.float32)
    return values * lax.rsqrt(jnp.mean(values * values, -1, keepdims=True) + 1e-06) * gain


def head_norm(values, heads):
    shaped = values.reshape(values.shape[:-1] + (heads, HD))
    return shaped * lax.rsqrt(jnp.mean(shaped * shaped, -1, keepdims=True) + 1e-06)


def attend_all(queries, keys_all, values_all, scales):
    cscores = (
        jnp.einsum("qhd,khd->hqk", queries, keys_all, preferred_element_type=jnp.float32)
        * (scales / HD)[:, None, None]
    )
    ctop = jnp.max(cscores, -1, keepdims=True)
    cexp = jnp.exp(cscores - ctop)
    cweights = (cexp / jnp.sum(cexp, -1, keepdims=True)).astype(jnp.bfloat16)
    return jnp.einsum(
        "hqk,khd->qhd", cweights, values_all, preferred_element_type=jnp.float32
    ).astype(jnp.bfloat16)


def shards(
    tokens,
    gain_attn,
    qkv_fine,
    scale_fine,
    out_fine,
    gain_ffn,
    ffn_in,
    ffn_out,
    up_proj,
    gain_coarse,
    qkv_coarse,
    scale_coarse,
    out_coarse,
):
    rows, cols, width = tokens.shape
    heads = width // HD
    count = rows * cols
    normed = rms_scale(tokens, gain_attn).astype(jnp.bfloat16).reshape(count, width)
    proj = jnp.dot(normed, qkv_fine, preferred_element_type=jnp.float32).reshape(
        rows, cols, 3 * width
    )
    query = head_norm(proj[..., :width], heads).astype(jnp.bfloat16).reshape(count, heads, HD)
    key_flat = head_norm(proj[..., width : 2 * width], heads).reshape(rows, cols, width)
    pairs = jnp.concatenate([key_flat, proj[..., 2 * width :]], -1).astype(jnp.bfloat16)
    padded = with_halo(pairs, (("ha", 0), ("wa", 1)), RADIUS)
    row_ids = lax.axis_index("ha") * rows + jnp.arange(rows + 2 * RADIUS, dtype=jnp.int32) - RADIUS
    col_ids = lax.axis_index("wa") * cols + jnp.arange(cols + 2 * RADIUS, dtype=jnp.int32) - RADIUS
    row_ok = (row_ids >= 0) & (row_ids < rows * lax.axis_size("ha"))
    col_ok = (col_ids >= 0) & (col_ids < cols * lax.axis_size("wa"))
    valid = row_ok[:, None] & col_ok[None, :]
    span = 2 * RADIUS + 1
    key_list = []
    value_list = []
    valid_list = []
    for shift_a in range(span):
        for shift_b in range(span):
            window = padded[shift_a : shift_a + rows, shift_b : shift_b + cols]
            key_list.append(window[..., :width])
            value_list.append(window[..., width:])
            valid_list.append(valid[shift_a : shift_a + rows, shift_b : shift_b + cols])
    key_stack = jnp.stack(key_list).reshape(span * span, count, heads, HD)
    value_stack = jnp.stack(value_list).reshape(span * span, count, heads, HD)
    valid_stack = jnp.stack(valid_list).reshape(span * span, count)
    raw = (
        jnp.einsum("nhd,snhd->hsn", query, key_stack, preferred_element_type=jnp.float32)
        * (scale_fine / HD)[:, None, None]
    )
    scores = jnp.where(valid_stack[None], raw, -1e30)
    top = jnp.max(scores, 1, keepdims=True)
    expo = jnp.exp(scores - top)
    weights = (expo / jnp.sum(expo, 1, keepdims=True)).astype(jnp.bfloat16)
    attn = jnp.einsum("hsn,snhd->nhd", weights, value_stack, preferred_element_type=jnp.float32)
    attn = attn.astype(jnp.bfloat16).reshape(count, width)
    h1 = (
        tokens.reshape(count, width).astype(jnp.float32)
        + jnp.dot(attn, out_fine, preferred_element_type=jnp.float32)
    ).astype(jnp.bfloat16)
    n2 = rms_scale(h1, gain_ffn).astype(jnp.bfloat16)
    mixed = jnp.dot(n2, ffn_in, preferred_element_type=jnp.float32)
    gated = (jax.nn.gelu(mixed[:, :FFH], approximate=True) * mixed[:, FFH:]).astype(jnp.bfloat16)
    fine_out = (
        h1.astype(jnp.float32) + jnp.dot(gated, ffn_out, preferred_element_type=jnp.float32)
    ).astype(jnp.bfloat16)
    fine_out = fine_out.reshape(rows, cols, width)
    rows_c, cols_c = (rows // POOL, cols // POOL)
    pooled = (
        fine_out.astype(jnp.float32).reshape(rows_c, POOL, cols_c, POOL, width).mean(axis=(1, 3))
    )
    pooled = pooled.astype(jnp.bfloat16).reshape(rows_c * cols_c, width)
    heads_c = CC // HD
    coarse = jnp.dot(pooled, up_proj, preferred_element_type=jnp.float32).astype(jnp.bfloat16)
    ncoarse = rms_scale(coarse, gain_coarse).astype(jnp.bfloat16)
    pc = jnp.dot(ncoarse, qkv_coarse, preferred_element_type=jnp.float32)
    cq = head_norm(pc[:, :CC], heads_c).astype(jnp.bfloat16)
    key_local = head_norm(pc[:, CC : 2 * CC], heads_c).astype(jnp.bfloat16)
    value_local = pc[:, 2 * CC :].reshape(-1, heads_c, HD).astype(jnp.bfloat16)
    group = heads_c // lax.axis_size("wa")
    group_scale = lax.dynamic_slice_in_dim(scale_coarse, lax.axis_index("wa") * group, group)
    query_grp, key_grp, value_grp = (
        lax.all_to_all(cq, "wa", split_axis=1, concat_axis=0, tiled=True),
        lax.all_to_all(key_local, "wa", split_axis=1, concat_axis=0, tiled=True),
        lax.all_to_all(value_local, "wa", split_axis=1, concat_axis=0, tiled=True),
    )
    key_every, value_every = (
        lax.all_gather(key_grp, "ha", axis=0, tiled=True),
        lax.all_gather(value_grp, "ha", axis=0, tiled=True),
    )
    result_grp = attend_all(query_grp, key_every, value_every, group_scale)
    cattn = lax.all_to_all(result_grp, "wa", split_axis=0, concat_axis=1, tiled=True).reshape(
        -1, CC
    )
    coarse_out = (
        coarse.astype(jnp.float32) + jnp.dot(cattn, out_coarse, preferred_element_type=jnp.float32)
    ).astype(jnp.bfloat16)
    return (fine_out, coarse_out.reshape(rows_c, cols_c, CC))


def solution(mesh):
    return jax.shard_map(
        shards,
        mesh=mesh,
        in_specs=(P("ha", "wa", None), P(), P(), P(), P(), P(), P(), P(), P(), P(), P(), P(), P()),
        out_specs=(P("ha", "wa", None), P("ha", "wa", None)),
        check_vma=False,
    )
```

profile of v0, /device:TPU:0, one launch (start us, length us, event | category | flops | bytes accessed | tf_op | source)
XLA Modules:
  0.0 476.4 jit_solution(6114502021061776474)
XLA Ops:
  6.9 2.1 mul.209
  12.6 3.6 collective-permute-start
  62.5 6.4 %collective-permute-start.2 = (bf16[22,3,512]{2,1,0:T(4,128)(2,1)}, bf16[22,3,512]{2,1,0:T(4,128)(2,1)}, u32[]{:S(2)}, u32[]{:S(2)}) collective-permute-start(bf16[22,3,512]{2,1,0:T(4,128)(2,1)} %get-tuple-element.94), channel_id=1, source_target_pairs={{0,1},{1,2},{2,3},{4,5},{5,6},{6,7},{8,9},{9,10},{10,11},{12,13},{... | collective-permute-start | bytes 202760 | tf_op jit(solution)/shard_map/ppermute | solution.py:21
  77.8 1.8 stack.538
  97.9 1.8 stack.504
  99.7 1.8 stack.505
  101.5 1.8 stack.506
  103.3 1.8 stack.507
  106.8 1.8 stack.509
  112.2 1.8 stack.513
  114.0 1.8 stack.514
  115.8 1.8 stack.515
  117.6 1.8 stack.516
  121.2 1.8 stack.519
  124.8 1.8 stack.521
  126.6 1.8 stack.522
  128.4 1.8 stack.523
  132.0 1.8 stack.526
  137.3 1.8 stack.529
  139.1 1.8 stack.530
  140.9 1.8 stack.532
  142.7 1.8 stack.533
  144.5 1.8 stack.534
  149.9 1.8 stack.537
  151.7 1.8 stack.539
  155.3 1.8 stack.541
  157.1 1.8 stack.542
  158.9 1.8 stack.543
  160.7 1.8 stack.544
  162.5 1.8 stack.546
  164.3 1.8 stack.547
  168.1 1.9 constant_dynamic-update-slice_fusion.47
  184.0 2.2 constant_dynamic-update-slice_fusion.38
  230.1 23.5 %fusion.1 = f32[4,256,1,49]{3,2,1,0:T(1,128)} fusion(bf16[49,256,4,64]{3,2,1,0:T(4,128)(2,1)} %constant_dynamic-update-slice_fusion, bf16[256,4,64,1]{2,1,0,3:T(4,128)(2,1)S(1)} %copy-done.48), kind=kOutput, calls=%fused_computation.2 | convolution fusion | flops 6422528 | bytes 6754304 | tf_op jit(solution)/shard_map/nhd,snhd->hsn/dot_general | solution.py:98
  256.1 5.1 %copy.46 = f32[256,4,49]{1,0,2:T(8,128)} copy(f32[256,4,49]{0,1,2:T(4,128)} %bitcast_convert_fusion) | data formatting | bytes 401408
  261.3 1.8 stack.550
  266.6 1.8 stack.552
  270.2 1.8 stack.555
  273.8 1.8 stack.557
  275.6 1.8 stack.558
  277.4 1.8 stack.559
  279.2 1.8 stack.561
  288.1 1.8 stack.566
  293.5 1.8 stack.570
  295.3 1.8 stack.571
  298.8 1.8 stack.573
  309.5 1.8 stack.580
  311.3 1.8 stack.582
  314.9 1.8 stack.584
  316.7 1.8 stack.585
  323.9 1.8 stack.590
  325.7 1.8 stack.591
  327.4 1.8 stack.592
  337.4 1.9 constant_dynamic-update-slice_fusion.96
  397.8 18.4 %multiply_reduce_fusion = bf16[256,4,64]{2,1,0:T(4,128)(2,1)S(1)} fusion(f32[256,4,49]{1,0,2:T(8,128)} %copy.46, bf16[49,256,4,64]{3,2,1,0:T(4,128)(2,1)} %constant_dynamic-update-slice_fusion.49), kind=kLoop, calls=%fused_computation.1 | loop fusion | flops 9568256 | bytes 6754304
  418.2 2.1 convert_reduce_fusion
  421.8 3.7 fusion.63
  427.5 4.3 all-to-all-start
  435.2 2.1 all-to-all-done
  437.3 3.2 all-to-all-start.2
  440.6 8.8 %all_gather.6 = bf16[32,4,64]{2,1,0:T(4,128)(2,1)S(1)} all-gather(bf16[4,4,64]{2,1,0:T(4,128)(2,1)S(1)} %bitcast.79), channel_id=1, replica_groups=mesh['ha'=8,'wa'=4] {'ha'}, dimensions={0}, use_global_device_ids=true | all-gather | bytes 18432 | tf_op jit(solution)/shard_map/all_gather | solution.py:139
  449.4 5.1 %all-to-all-start.1 = ((bf16[4,2,128]{2,1,0:T(2,128)(2,1)}), bf16[4,2,128]{2,1,0:T(2,128)(2,1)S(1)}, u32[]{:S(2)}, u32[]{:S(2)}) async-start(bf16[4,2,128]{2,1,0:T(2,128)(2,1)} %reshape.623), calls=%async_computation.1 | async-start | bytes 4096 | tf_op jit(solution)/shard_map/all_to_all | solution.py:133
  454.6 9.2 %all_gather.7 = bf16[32,4,64]{2,1,0:T(4,128)(2,1)S(1)} all-gather(bf16[4,4,64]{2,1,0:T(4,128)(2,1)S(1)} %bitcast.80), channel_id=1, replica_groups=mesh['ha'=8,'wa'=4] {'ha'}, dimensions={0}, use_global_device_ids=true | all-gather | bytes 18432 | tf_op jit(solution)/shard_map/all_gather | solution.py:138
  464.5 10.4 %all_to_all.45 = bf16[4,2,128]{2,1,0:T(2,128)(2,1)S(1)} all-to-all(bf16[4,2,128]{2,1,0:T(2,128)(2,1)S(1)} %reshape.625), channel_id=1, replica_groups=mesh['ha'=8,'wa'=4] {'wa'}, dimensions={0} | all-to-all | bytes 4096 | tf_op jit(solution)/shard_map/all_to_all | solution.py:142
  (393 shorter events, 277.0 us)
Async XLA Ops:
  0.6 474.5 %copy-start = (bf16[1024,1024]{1,0:T(8,128)(2,1)S(1)}, bf16[1024,1024]{1,0:T(8,128)(2,1)}, u32[]{:S(2)}) copy-start(bf16[1024,1024]{1,0:T(8,128)(2,1)} %param.25) | copy-start | bytes 6291460
  11.3 48.3 %collective-permute-start.1 = (bf16[3,16,512]{2,1,0:T(8,128)(2,1)}, bf16[3,16,512]{2,1,0:T(8,128)(2,1)}, u32[]{:S(2)}, u32[]{:S(2)}) collective-permute-start(bf16[3,16,512]{2,1,0:T(8,128)(2,1)} %get-tuple-element.110), channel_id=1, source_target_pairs={{4,0},{8,4},{12,8},{16,12},{20,16},{24,20},{28,24},{5,1},{9,5},{13... | collective-permute-start | bytes 147464 | tf_op jit(solution)/shard_map/ppermute | solution.py:23
  12.6 47.1 %collective-permute-start = (bf16[3,16,512]{2,1,0:T(8,128)(2,1)}, bf16[3,16,512]{2,1,0:T(8,128)(2,1)}, u32[]{:S(2)}, u32[]{:S(2)}) collective-permute-start(bf16[3,16,512]{2,1,0:T(8,128)(2,1)} %get-tuple-element.109), channel_id=1, source_target_pairs={{0,4},{4,8},{8,12},{12,16},{16,20},{20,24},{24,28},{1,5},{5,9},{9,... | collective-permute-start | bytes 147464 | tf_op jit(solution)/shard_map/ppermute | solution.py:21
  61.2 22.4 %collective-permute-start.3 = (bf16[22,3,512]{2,1,0:T(4,128)(2,1)}, bf16[22,3,512]{2,1,0:T(4,128)(2,1)}, u32[]{:S(2)}, u32[]{:S(2)}) collective-permute-start(bf16[22,3,512]{2,1,0:T(4,128)(2,1)} %get-tuple-element.93), channel_id=1, source_target_pairs={{1,0},{2,1},{3,2},{5,4},{6,5},{7,6},{9,8},{10,9},{11,10},{13,12},{... | collective-permute-start | bytes 202760 | tf_op jit(solution)/shard_map/ppermute | solution.py:23
  62.5 21.1 %collective-permute-start.2 = (bf16[22,3,512]{2,1,0:T(4,128)(2,1)}, bf16[22,3,512]{2,1,0:T(4,128)(2,1)}, u32[]{:S(2)}, u32[]{:S(2)}) collective-permute-start(bf16[22,3,512]{2,1,0:T(4,128)(2,1)} %get-tuple-element.94), channel_id=1, source_target_pairs={{0,1},{1,2},{2,3},{4,5},{5,6},{6,7},{8,9},{9,10},{10,11},{12,13},{... | collective-permute-start | bytes 202760 | tf_op jit(solution)/shard_map/ppermute | solution.py:21
  106.8 102.1 %copy-start.3 = (bf16[1,256,4,64]{3,2,1,0:T(4,128)(2,1)S(1)}, bf16[1,256,4,64]{3,2,1,0:T(4,128)(2,1)}, u32[]{:S(2)}) copy-start(bf16[1,256,4,64]{3,2,1,0:T(4,128)(2,1)} %stack.524) | copy-start | bytes 393220
  167.9 43.7 %copy-start.46 = (bf16[1,256,4,64]{3,2,1,0:T(4,128)(2,1)S(1)}, bf16[1,256,4,64]{3,2,1,0:T(4,128)(2,1)}, u32[]{:S(2)}) copy-start(bf16[1,256,4,64]{3,2,1,0:T(4,128)(2,1)} %stack.526) | copy-start | bytes 393220
  167.9 44.5 %copy-start.45 = (bf16[1,256,4,64]{3,2,1,0:T(4,128)(2,1)S(1)}, bf16[1,256,4,64]{3,2,1,0:T(4,128)(2,1)}, u32[]{:S(2)}) copy-start(bf16[1,256,4,64]{3,2,1,0:T(4,128)(2,1)} %stack.527) | copy-start | bytes 393220
  167.9 45.3 %copy-start.43 = (bf16[1,256,4,64]{3,2,1,0:T(4,128)(2,1)S(1)}, bf16[1,256,4,64]{3,2,1,0:T(4,128)(2,1)}, u32[]{:S(2)}) copy-start(bf16[1,256,4,64]{3,2,1,0:T(4,128)(2,1)} %stack.528) | copy-start | bytes 393220
  167.9 46.1 %copy-start.41 = (bf16[1,256,4,64]{3,2,1,0:T(4,128)(2,1)S(1)}, bf16[1,256,4,64]{3,2,1,0:T(4,128)(2,1)}, u32[]{:S(2)}) copy-start(bf16[1,256,4,64]{3,2,1,0:T(4,128)(2,1)} %stack.529) | copy-start | bytes 393220
  167.9 46.9 %copy-start.39 = (bf16[1,256,4,64]{3,2,1,0:T(4,128)(2,1)S(1)}, bf16[1,256,4,64]{3,2,1,0:T(4,128)(2,1)}, u32[]{:S(2)}) copy-start(bf16[1,256,4,64]{3,2,1,0:T(4,128)(2,1)} %stack.530) | copy-start | bytes 393220
  167.9 47.7 %copy-start.6 = (bf16[1,256,4,64]{3,2,1,0:T(4,128)(2,1)S(1)}, bf16[1,256,4,64]{3,2,1,0:T(4,128)(2,1)}, u32[]{:S(2)}) copy-start(bf16[1,256,4,64]{3,2,1,0:T(4,128)(2,1)} %stack.531) | copy-start | bytes 393220
  167.9 48.5 %copy-start.36 = (bf16[1,256,4,64]{3,2,1,0:T(4,128)(2,1)S(1)}, bf16[1,256,4,64]{3,2,1,0:T(4,128)(2,1)}, u32[]{:S(2)}) copy-start(bf16[1,256,4,64]{3,2,1,0:T(4,128)(2,1)} %stack.532) | copy-start | bytes 393220
  167.9 49.3 %copy-start.35 = (bf16[1,256,4,64]{3,2,1,0:T(4,128)(2,1)S(1)}, bf16[1,256,4,64]{3,2,1,0:T(4,128)(2,1)}, u32[]{:S(2)}) copy-start(bf16[1,256,4,64]{3,2,1,0:T(4,128)(2,1)} %stack.533) | copy-start | bytes 393220
  167.9 50.1 %copy-start.33 = (bf16[1,256,4,64]{3,2,1,0:T(4,128)(2,1)S(1)}, bf16[1,256,4,64]{3,2,1,0:T(4,128)(2,1)}, u32[]{:S(2)}) copy-start(bf16[1,256,4,64]{3,2,1,0:T(4,128)(2,1)} %stack.534) | copy-start | bytes 393220
  167.9 50.9 %copy-start.31 = (bf16[1,256,4,64]{3,2,1,0:T(4,128)(2,1)S(1)}, bf16[1,256,4,64]{3,2,1,0:T(4,128)(2,1)}, u32[]{:S(2)}) copy-start(bf16[1,256,4,64]{3,2,1,0:T(4,128)(2,1)} %stack.535) | copy-start | bytes 393220
  167.9 51.6 %copy-start.29 = (bf16[1,256,4,64]{3,2,1,0:T(4,128)(2,1)S(1)}, bf16[1,256,4,64]{3,2,1,0:T(4,128)(2,1)}, u32[]{:S(2)}) copy-start(bf16[1,256,4,64]{3,2,1,0:T(4,128)(2,1)} %stack.536) | copy-start | bytes 393220
  167.9 52.4 %copy-start.27 = (bf16[1,256,4,64]{3,2,1,0:T(4,128)(2,1)S(1)}, bf16[1,256,4,64]{3,2,1,0:T(4,128)(2,1)}, u32[]{:S(2)}) copy-start(bf16[1,256,4,64]{3,2,1,0:T(4,128)(2,1)} %stack.537) | copy-start | bytes 393220
  167.9 53.2 %copy-start.5 = (bf16[1,256,4,64]{3,2,1,0:T(4,128)(2,1)S(1)}, bf16[1,256,4,64]{3,2,1,0:T(4,128)(2,1)}, u32[]{:S(2)}) copy-start(bf16[1,256,4,64]{3,2,1,0:T(4,128)(2,1)} %stack.538) | copy-start | bytes 393220
  168.0 54.1 %copy-start.24 = (bf16[1,256,4,64]{3,2,1,0:T(4,128)(2,1)S(1)}, bf16[1,256,4,64]{3,2,1,0:T(4,128)(2,1)}, u32[]{:S(2)}) copy-start(bf16[1,256,4,64]{3,2,1,0:T(4,128)(2,1)} %stack.539) | copy-start | bytes 393220
  168.0 54.8 %copy-start.23 = (bf16[1,256,4,64]{3,2,1,0:T(4,128)(2,1)S(1)}, bf16[1,256,4,64]{3,2,1,0:T(4,128)(2,1)}, u32[]{:S(2)}) copy-start(bf16[1,256,4,64]{3,2,1,0:T(4,128)(2,1)} %stack.540) | copy-start | bytes 393220
  168.0 55.6 %copy-start.21 = (bf16[1,256,4,64]{3,2,1,0:T(4,128)(2,1)S(1)}, bf16[1,256,4,64]{3,2,1,0:T(4,128)(2,1)}, u32[]{:S(2)}) copy-start(bf16[1,256,4,64]{3,2,1,0:T(4,128)(2,1)} %stack.541) | copy-start | bytes 393220
  168.0 56.5 %copy-start.19 = (bf16[1,256,4,64]{3,2,1,0:T(4,128)(2,1)S(1)}, bf16[1,256,4,64]{3,2,1,0:T(4,128)(2,1)}, u32[]{:S(2)}) copy-start(bf16[1,256,4,64]{3,2,1,0:T(4,128)(2,1)} %stack.542) | copy-start | bytes 393220
  168.0 57.3 %copy-start.17 = (bf16[1,256,4,64]{3,2,1,0:T(4,128)(2,1)S(1)}, bf16[1,256,4,64]{3,2,1,0:T(4,128)(2,1)}, u32[]{:S(2)}) copy-start(bf16[1,256,4,64]{3,2,1,0:T(4,128)(2,1)} %stack.543) | copy-start | bytes 393220
  168.0 58.1 %copy-start.15 = (bf16[1,256,4,64]{3,2,1,0:T(4,128)(2,1)S(1)}, bf16[1,256,4,64]{3,2,1,0:T(4,128)(2,1)}, u32[]{:S(2)}) copy-start(bf16[1,256,4,64]{3,2,1,0:T(4,128)(2,1)} %stack.544) | copy-start | bytes 393220
  168.0 58.9 %copy-start.4 = (bf16[1,256,4,64]{3,2,1,0:T(4,128)(2,1)S(1)}, bf16[1,256,4,64]{3,2,1,0:T(4,128)(2,1)}, u32[]{:S(2)}) copy-start(bf16[1,256,4,64]{3,2,1,0:T(4,128)(2,1)} %stack.545) | copy-start | bytes 393220
  168.0 59.7 %copy-start.12 = (bf16[1,256,4,64]{3,2,1,0:T(4,128)(2,1)S(1)}, bf16[1,256,4,64]{3,2,1,0:T(4,128)(2,1)}, u32[]{:S(2)}) copy-start(bf16[1,256,4,64]{3,2,1,0:T(4,128)(2,1)} %stack.546) | copy-start | bytes 393220
  168.0 60.5 %copy-start.10 = (bf16[1,256,4,64]{3,2,1,0:T(4,128)(2,1)S(1)}, bf16[1,256,4,64]{3,2,1,0:T(4,128)(2,1)}, u32[]{:S(2)}) copy-start(bf16[1,256,4,64]{3,2,1,0:T(4,128)(2,1)} %stack.547) | copy-start | bytes 393220
  168.0 61.2 %copy-start.7 = (bf16[1,256,4,64]{3,2,1,0:T(4,128)(2,1)S(1)}, bf16[1,256,4,64]{3,2,1,0:T(4,128)(2,1)}, u32[]{:S(2)}) copy-start(bf16[1,256,4,64]{3,2,1,0:T(4,128)(2,1)} %stack.548) | copy-start | bytes 393220
  168.1 62.0 %copy-start.48 = (bf16[256,4,64,1]{2,1,0,3:T(4,128)(2,1)S(1)}, bf16[256,4,64,1]{2,1,0,3:T(4,128)(2,1)}, u32[]{:S(2)}) copy-start(bf16[256,4,64,1]{2,1,0,3:T(4,128)(2,1)} %fusion.26) | copy-start | bytes 393220
  226.9 28.0 %copy-start.50 = (f32[4]{0:T(128)S(1)}, f32[4]{0:T(128)}, u32[]{:S(2)}) copy-start(f32[4]{0:T(128)} %broadcast_multiply_fusion) | copy-start | bytes 52
  261.3 104.2 %copy-start.2 = (bf16[1,256,4,64]{3,2,1,0:T(4,128)(2,1)S(1)}, bf16[1,256,4,64]{3,2,1,0:T(4,128)(2,1)}, u32[]{:S(2)}) copy-start(bf16[1,256,4,64]{3,2,1,0:T(4,128)(2,1)} %stack.567) | copy-start | bytes 393220
  337.2 42.0 %copy-start.44 = (bf16[1,256,4,64]{3,2,1,0:T(4,128)(2,1)S(1)}, bf16[1,256,4,64]{3,2,1,0:T(4,128)(2,1)}, u32[]{:S(2)}) copy-start(bf16[1,256,4,64]{3,2,1,0:T(4,128)(2,1)} %stack.576) | copy-start | bytes 393220
  337.2 42.8 %copy-start.42 = (bf16[1,256,4,64]{3,2,1,0:T(4,128)(2,1)S(1)}, bf16[1,256,4,64]{3,2,1,0:T(4,128)(2,1)}, u32[]{:S(2)}) copy-start(bf16[1,256,4,64]{3,2,1,0:T(4,128)(2,1)} %stack.577) | copy-start | bytes 393220
  337.2 43.6 %copy-start.40 = (bf16[1,256,4,64]{3,2,1,0:T(4,128)(2,1)S(1)}, bf16[1,256,4,64]{3,2,1,0:T(4,128)(2,1)}, u32[]{:S(2)}) copy-start(bf16[1,256,4,64]{3,2,1,0:T(4,128)(2,1)} %stack.578) | copy-start | bytes 393220
  337.2 44.5 %copy-start.38 = (bf16[1,256,4,64]{3,2,1,0:T(4,128)(2,1)S(1)}, bf16[1,256,4,64]{3,2,1,0:T(4,128)(2,1)}, u32[]{:S(2)}) copy-start(bf16[1,256,4,64]{3,2,1,0:T(4,128)(2,1)} %stack.579) | copy-start | bytes 393220
  337.2 45.2 %copy-start.37 = (bf16[1,256,4,64]{3,2,1,0:T(4,128)(2,1)S(1)}, bf16[1,256,4,64]{3,2,1,0:T(4,128)(2,1)}, u32[]{:S(2)}) copy-start(bf16[1,256,4,64]{3,2,1,0:T(4,128)(2,1)} %stack.580) | copy-start | bytes 393220
  337.2 46.9 %copy-start.34 = (bf16[1,256,4,64]{3,2,1,0:T(4,128)(2,1)S(1)}, bf16[1,256,4,64]{3,2,1,0:T(4,128)(2,1)}, u32[]{:S(2)}) copy-start(bf16[1,256,4,64]{3,2,1,0:T(4,128)(2,1)} %stack.582) | copy-start | bytes 393220
  337.2 47.6 %copy-start.32 = (bf16[1,256,4,64]{3,2,1,0:T(4,128)(2,1)S(1)}, bf16[1,256,4,64]{3,2,1,0:T(4,128)(2,1)}, u32[]{:S(2)}) copy-start(bf16[1,256,4,64]{3,2,1,0:T(4,128)(2,1)} %stack.583) | copy-start | bytes 393220
  337.3 48.4 %copy-start.30 = (bf16[1,256,4,64]{3,2,1,0:T(4,128)(2,1)S(1)}, bf16[1,256,4,64]{3,2,1,0:T(4,128)(2,1)}, u32[]{:S(2)}) copy-start(bf16[1,256,4,64]{3,2,1,0:T(4,128)(2,1)} %stack.584) | copy-start | bytes 393220
  337.3 49.2 %copy-start.28 = (bf16[1,256,4,64]{3,2,1,0:T(4,128)(2,1)S(1)}, bf16[1,256,4,64]{3,2,1,0:T(4,128)(2,1)}, u32[]{:S(2)}) copy-start(bf16[1,256,4,64]{3,2,1,0:T(4,128)(2,1)} %stack.585) | copy-start | bytes 393220
  337.3 50.0 %copy-start.26 = (bf16[1,256,4,64]{3,2,1,0:T(4,128)(2,1)S(1)}, bf16[1,256,4,64]{3,2,1,0:T(4,128)(2,1)}, u32[]{:S(2)}) copy-start(bf16[1,256,4,64]{3,2,1,0:T(4,128)(2,1)} %stack.586) | copy-start | bytes 393220
  337.3 50.8 %copy-start.25 = (bf16[1,256,4,64]{3,2,1,0:T(4,128)(2,1)S(1)}, bf16[1,256,4,64]{3,2,1,0:T(4,128)(2,1)}, u32[]{:S(2)}) copy-start(bf16[1,256,4,64]{3,2,1,0:T(4,128)(2,1)} %stack.587) | copy-start | bytes 393220
  337.3 52.4 %copy-start.22 = (bf16[1,256,4,64]{3,2,1,0:T(4,128)(2,1)S(1)}, bf16[1,256,4,64]{3,2,1,0:T(4,128)(2,1)}, u32[]{:S(2)}) copy-start(bf16[1,256,4,64]{3,2,1,0:T(4,128)(2,1)} %stack.589) | copy-start | bytes 393220
  337.3 53.2 %copy-start.20 = (bf16[1,256,4,64]{3,2,1,0:T(4,128)(2,1)S(1)}, bf16[1,256,4,64]{3,2,1,0:T(4,128)(2,1)}, u32[]{:S(2)}) copy-start(bf16[1,256,4,64]{3,2,1,0:T(4,128)(2,1)} %stack.590) | copy-start | bytes 393220
  337.3 53.9 %copy-start.18 = (bf16[1,256,4,64]{3,2,1,0:T(4,128)(2,1)S(1)}, bf16[1,256,4,64]{3,2,1,0:T(4,128)(2,1)}, u32[]{:S(2)}) copy-start(bf16[1,256,4,64]{3,2,1,0:T(4,128)(2,1)} %stack.591) | copy-start | bytes 393220
  337.3 54.8 %copy-start.16 = (bf16[1,256,4,64]{3,2,1,0:T(4,128)(2,1)S(1)}, bf16[1,256,4,64]{3,2,1,0:T(4,128)(2,1)}, u32[]{:S(2)}) copy-start(bf16[1,256,4,64]{3,2,1,0:T(4,128)(2,1)} %stack.592) | copy-start | bytes 393220
  337.3 55.6 %copy-start.13 = (bf16[1,256,4,64]{3,2,1,0:T(4,128)(2,1)S(1)}, bf16[1,256,4,64]{3,2,1,0:T(4,128)(2,1)}, u32[]{:S(2)}) copy-start(bf16[1,256,4,64]{3,2,1,0:T(4,128)(2,1)} %stack.593) | copy-start | bytes 393220
  337.3 56.4 %copy-start.14 = (bf16[1,256,4,64]{3,2,1,0:T(4,128)(2,1)S(1)}, bf16[1,256,4,64]{3,2,1,0:T(4,128)(2,1)}, u32[]{:S(2)}) copy-start(bf16[1,256,4,64]{3,2,1,0:T(4,128)(2,1)} %stack.594) | copy-start | bytes 393220
  337.4 58.0 %copy-start.11 = (bf16[1,256,4,64]{3,2,1,0:T(4,128)(2,1)S(1)}, bf16[1,256,4,64]{3,2,1,0:T(4,128)(2,1)}, u32[]{:S(2)}) copy-start(bf16[1,256,4,64]{3,2,1,0:T(4,128)(2,1)} %stack.596) | copy-start | bytes 393220
  337.4 58.8 %copy-start.8 = (bf16[1,256,4,64]{3,2,1,0:T(4,128)(2,1)S(1)}, bf16[1,256,4,64]{3,2,1,0:T(4,128)(2,1)}, u32[]{:S(2)}) copy-start(bf16[1,256,4,64]{3,2,1,0:T(4,128)(2,1)} %stack.597) | copy-start | bytes 393220
  337.4 59.6 %copy-start.9 = (bf16[1,256,4,64]{3,2,1,0:T(4,128)(2,1)S(1)}, bf16[1,256,4,64]{3,2,1,0:T(4,128)(2,1)}, u32[]{:S(2)}) copy-start(bf16[1,256,4,64]{3,2,1,0:T(4,128)(2,1)} %stack.598) | copy-start | bytes 393220
  388.9 27.4 %copy-start.1 = (bf16[16,16,256]{2,1,0:T(8,128)(2,1)S(1)}, bf16[16,16,256]{2,1,0:T(8,128)(2,1)}, u32[]{:S(2)}) copy-start(bf16[16,16,256]{2,1,0:T(8,128)(2,1)} %param.13) | copy-start | bytes 393220
  388.9 27.4 %copy-start.49 = (bf16[256,256]{1,0:T(8,128)(2,1)S(1)}, bf16[256,256]{1,0:T(8,128)(2,1)}, u32[]{:S(2)}) copy-start(bf16[256,256]{1,0:T(8,128)(2,1)} %param.17) | copy-start | bytes 393220
  389.7 27.0 %copy-start.52 = (f32[256]{0:T(256)S(1)}, f32[256]{0:T(256)}, u32[]{:S(2)}) copy-start(f32[256]{0:T(256)} %param.18) | copy-start | bytes 3076
  397.8 22.5 %copy-start.47 = (bf16[256,1024]{1,0:T(8,128)(2,1)S(1)}, bf16[256,1024]{1,0:T(8,128)(2,1)}, u32[]{:S(2)}) copy-start(bf16[256,1024]{1,0:T(8,128)(2,1)} %param.21) | copy-start | bytes 1572868
  397.8 24.0 %copy-start.51 = (f32[1024]{0:T(1024)S(1)}, f32[1024]{0:T(1024)}, u32[]{:S(2)}) copy-start(f32[1024]{0:T(1024)} %param.22) | copy-start | bytes 12292
  397.8 66.2 %copy-start.53 = (f32[4]{0:T(128)S(1)}, f32[4]{0:T(128)}, u32[]{:S(2)}) copy-start(f32[4]{0:T(128)} %dynamic-slice_multiply_fusion) | copy-start | bytes 52
  427.5 9.8 %all-to-all-start = ((bf16[4,2,128]{2,1,0:T(2,128)(2,1)}), bf16[4,2,128]{2,1,0:T(2,128)(2,1)S(1)}, u32[]{:S(2)}, u32[]{:S(2)}) async-start(bf16[4,2,128]{2,1,0:T(2,128)(2,1)} %reshape.619), calls=%async_computation | async-start | bytes 4096 | tf_op jit(solution)/shard_map/all_to_all | solution.py:135
  437.3 12.2 %all-to-all-start.2 = ((bf16[4,2,128]{2,1,0:T(2,128)(2,1)}), bf16[4,2,128]{2,1,0:T(2,128)(2,1)S(1)}, u32[]{:S(2)}, u32[]{:S(2)}) async-start(bf16[4,2,128]{2,1,0:T(2,128)(2,1)} %reshape.621), calls=%async_computation.2 | async-start | bytes 4096 | tf_op jit(solution)/shard_map/all_to_all | solution.py:134
  449.4 14.4 %all-to-all-start.1 = ((bf16[4,2,128]{2,1,0:T(2,128)(2,1)}), bf16[4,2,128]{2,1,0:T(2,128)(2,1)S(1)}, u32[]{:S(2)}, u32[]{:S(2)}) async-start(bf16[4,2,128]{2,1,0:T(2,128)(2,1)} %reshape.623), calls=%async_computation.1 | async-start | bytes 4096 | tf_op jit(solution)/shard_map/all_to_all | solution.py:133
where the time goes:
time: 486 us; the launch traced here: 476 us
  local copies, waits for them, and re-layouts  349 us (72%)
  other arithmetic  35.7 us (7%)
  matrix products  33.4 us (7%)
  blocking collectives  28.5 us (6%)
  starting transfers between devices  25.2 us (5%)
    unnamed x217, local copies, waits for them, and re-layouts  131 us
    another operation x50, local copies, waits for them, and re-layouts, shards(): key_stack = jnp.stack(key_list).reshape(span * span, count, heads, HD)  86.1 us
    another operation x50, local copies, waits for them, and re-layouts, shards(): value_stack = jnp.stack(value_list).reshape(span * span, count, heads, HD)  78.2 us
    another operation x50, local copies, waits for them, and re-layouts, shards(): valid_stack = jnp.stack(valid_list).reshape(span * span, count)  34.7 us
    dot_general x1, matrix products, shards(): jnp.einsum('nhd,snhd->hsn', query, key_stack, preferred_element_type=jnp....  23.5 us
    unnamed x7, other arithmetic  21.4 us
    all_to_all x1, blocking collectives, shards(): lax.all_to_all(result_grp, 'wa', split_axis=0, concat_axis=1, tiled=True)  10.4 us
    ppermute x2, starting transfers between devices, with_halo(): lax.ppermute(tail, axis, [(i, (i + 1) % count) for i in range(ends)])  10.1 us
  transfers between devices with their start and end apart: 7, of which 1 were waited for; matrix products, arithmetic and copies ran while one was open for 13% of the time, Pallas kernels for 0%

commit v1 on v0

v1 whole, which is shorter than its diff:
```python
import functools

import jax
import jax.numpy as jnp
from jax import lax
from jax.experimental import pallas as pl
from jax.experimental.pallas import tpu as pltpu
from jax.sharding import PartitionSpec as P

HD = 64
RADIUS = 3
LOG2E = 1.4426950408889634
BIG = 2.0**30
BF = jnp.bfloat16
F32 = jnp.float32
MIB = 1 << 20


def rounded_up(value, step):
    return -(-value // step) * step


def dot(a, b):
    return jnp.dot(a, b, preferred_element_type=F32)


def dot_nt(a, b):
    return lax.dot_general(a, b, (((1,), (1,)), ((), ())), preferred_element_type=F32)


def dot_split(values, ones):
    high = values.astype(BF)
    low = (values - high.astype(F32)).astype(BF)
    return dot(high, ones) + dot(low, ones)


def same_head(rows, cols):
    shape = (rows, cols)
    left = lax.broadcasted_iota(jnp.int32, shape, 0) // HD
    right = lax.broadcasted_iota(jnp.int32, shape, 1) // HD
    return (left == right).astype(F32).astype(BF)


def head_norm(values, ones):
    return values * lax.rsqrt(dot_split(values * values, ones) * (1.0 / HD) + 1e-06)


def rms_norm(values, gain):
    mean = jnp.mean(values * values, -1, keepdims=True)
    return values * lax.rsqrt(mean + 1e-06) * gain


def edge_kernel(rows, cols, tok_ref, up_ref, down_ref, left_ref, right_ref):
    height = rows + 2 * RADIUS
    strip = RADIUS * cols
    padded = left_ref.shape[0]
    block = jnp.concatenate([up_ref[...], tok_ref[...], down_ref[...]], 0)
    out = lax.broadcasted_iota(jnp.int32, (padded, block.shape[0]), 0)
    src = lax.broadcasted_iota(jnp.int32, (padded, block.shape[0]), 1)
    row = (out * 21846) >> 16
    first = row * cols + (out - 3 * row)
    inside = out < height * RADIUS
    pick = jnp.where(inside & (src == first), 1.0, 0.0).astype(BF)
    left_ref[...] = dot(pick, block).astype(BF)
    pick = jnp.where(inside & (src == first + (cols - RADIUS)), 1.0, 0.0).astype(BF)
    right_ref[...] = dot(pick, block).astype(BF)


def fine_kernel(
    rows, cols, heads, axes,
    tok_ref, up_ref, down_ref, left_ref, right_ref, gain_attn_ref, qkv_ref, scale_ref,
    out_ref, gain_ffn_ref, ffn_in_ref, ffn_out_ref,
    fine_ref, pooled_ref,
):
    count = rows * cols
    strip = RADIUS * cols
    side = left_ref.shape[0]
    width = heads * HD
    total = count + 2 * strip + 2 * side
    row_axis, col_axis = axes
    row0 = lax.axis_index(row_axis) * rows
    col0 = lax.axis_index(col_axis) * cols
    grid_rows = lax.axis_size(row_axis) * rows
    grid_cols = lax.axis_size(col_axis) * cols

    gain = gain_attn_ref[...]
    tok = tok_ref[...].astype(F32)
    halo = jnp.concatenate([up_ref[...], down_ref[...], left_ref[...], right_ref[...]], 0)
    normed = rms_norm(tok, gain).astype(BF)
    normed_halo = rms_norm(halo.astype(F32), gain).astype(BF)
    ones = same_head(width, width)
    query = head_norm(dot(normed, qkv_ref[:, :width]), ones).astype(BF)
    every = jnp.concatenate([normed, normed_halo], 0)
    key = head_norm(dot(every, qkv_ref[:, width : 2 * width]), ones).astype(BF)
    value = dot(every, qkv_ref[:, 2 * width :]).astype(BF)

    lanes = 2 * HD
    spot = lax.broadcasted_iota(jnp.int32, (total, 1), 0)
    past_own = spot - count
    past_up = past_own - strip
    past_down = past_up - strip
    past_left = past_down - side
    side_at = jnp.where(past_left >= 0, past_left, past_down)
    side_row = (side_at * 21846) >> 16
    side_col = side_at - 3 * side_row - RADIUS
    strip_at = jnp.where(past_up >= 0, past_up, past_own)
    in_own = past_own < 0
    in_strip = past_down < 0
    krow = jnp.where(
        in_own,
        spot // cols,
        jnp.where(
            in_strip,
            strip_at // cols + jnp.where(past_up >= 0, rows, -RADIUS),
            side_row - RADIUS,
        ),
    )
    kcol = jnp.where(
        in_own,
        spot % cols,
        jnp.where(in_strip, strip_at % cols, side_col + jnp.where(past_left >= 0, cols + RADIUS, 0)),
    )
    real = in_strip | (side_at < (rows + 2 * RADIUS) * RADIUS)
    real = real & (krow + row0 >= 0) & (krow + row0 < grid_rows)
    real = real & (kcol + col0 >= 0) & (kcol + col0 < grid_cols)
    krow = jnp.where(real, krow, -1000)

    lane = lax.broadcasted_iota(jnp.int32, (1, lanes), 1)
    place = lane % HD
    is_row = place < rows
    is_col = (place >= rows) & (place < rows + cols)
    far_row = jnp.abs(krow - place) > RADIUS
    far_col = jnp.abs(kcol - (place - rows)) > RADIUS
    key_mask = jnp.where((is_row & far_row) | (is_col & far_col), -BIG, 0.0).astype(BF)
    qspot = lax.broadcasted_iota(jnp.int32, (count, 1), 0)
    hot = (is_row & (qspot // cols == place)) | (is_col & (qspot % cols == place - rows))
    query_mask = jnp.where(hot, 1.0, 0.0).astype(BF)

    low_half = lane < HD
    one = jnp.ones((1, lanes), BF)
    parts = []
    for pair in range(heads // 2):
        span = slice(pair * lanes, (pair + 1) * lanes)
        sums = []
        for half in range(2):
            mine = low_half if half == 0 else ~low_half
            q = jnp.where(mine, query[:, span], query_mask)
            k = jnp.where(mine, key[:, span], key_mask)
            v = jnp.where(mine, value[:, span], one)
            factor = scale_ref[2 * pair + half] * (LOG2E / HD)
            weights = jnp.exp2(dot_nt(q, k) * factor).astype(BF)
            sums.append(dot(weights, v))
        top = jnp.where(low_half, sums[0], sums[1])
        bottom = pltpu.roll(jnp.where(low_half, sums[1], sums[0]), HD, 1)
        parts.append((top / bottom).astype(BF))
    attn = jnp.concatenate(parts, 1)

    h1 = (tok + dot(attn, out_ref[...])).astype(BF)
    h1_wide = h1.astype(F32)
    n2 = rms_norm(h1_wide, gain_ffn_ref[...]).astype(BF)
    hidden = ffn_out_ref.shape[0]
    gate = dot(n2, ffn_in_ref[:, :hidden])
    up = dot(n2, ffn_in_ref[:, hidden:])
    gated = (jax.nn.gelu(gate, approximate=True) * up).astype(BF)
    fine = (h1_wide + dot(gated, ffn_out_ref[...])).astype(BF)
    fine_ref[...] = fine
    pooled_ref[...] = jnp.mean(fine.astype(F32), 0, keepdims=True).astype(BF)


def coarse_kernel(
    heads, axes,
    pooled_ref, up_ref, gain_ref, qkv_ref, scale_ref, out_ref,
    coarse_out_ref,
    query_ref, coarse_ref,
):
    width = heads * HD
    row_axis, col_axis = axes
    mine = lax.axis_index(row_axis) * lax.axis_size(col_axis) + lax.axis_index(col_axis)
    coarse = dot(pooled_ref[...], up_ref[...]).astype(BF).astype(F32)
    coarse_ref[...] = coarse
    normed = rms_norm(coarse, gain_ref[...]).astype(BF)
    group = 4 * HD
    ones = same_head(group, group)
    keys = []
    for at in range(0, width, group):
        span = slice(at, at + group)
        query_ref[:, span] = head_norm(dot(normed, qkv_ref[:, span]), ones).astype(BF).astype(F32)
        keys.append(head_norm(dot(normed, qkv_ref[:, width + at : width + at + group]), ones))
    key = jnp.concatenate(keys, 1).astype(BF).astype(F32)
    value = dot(normed, qkv_ref[:, 2 * width :]).astype(BF).astype(F32)
    query = query_ref[pl.ds(mine, 1), :]
    lanes = 2 * HD
    scale = jnp.zeros((1, lanes), F32)
    lane = lax.broadcasted_iota(jnp.int32, (1, lanes), 1)
    for head in range(heads):
        scale = jnp.where(lane == head, scale_ref[head], scale)
    shape = (width, lanes)
    fold = lax.broadcasted_iota(jnp.int32, shape, 0) // HD == lax.broadcasted_iota(jnp.int32, shape, 1)
    fold = fold.astype(F32).astype(BF)
    scores = dot_split(key * query, fold) * (scale * (1.0 / HD))
    expo = jnp.exp(scores - jnp.max(scores, 0, keepdims=True))
    weights = (expo / jnp.sum(expo, 0, keepdims=True)).astype(BF)
    spread = dot_nt(weights, fold)
    cattn = jnp.sum(spread * value, 0, keepdims=True).astype(BF)
    coarse_out_ref[...] = (coarse_ref[pl.ds(mine, 1), :] + dot(cattn, out_ref[...])).astype(BF)


def vmem():
    return pl.BlockSpec(memory_space=pltpu.VMEM)


def smem():
    return pl.BlockSpec(memory_space=pltpu.SMEM)


def in_vmem(array):
    return pltpu.with_memory_space_constraint(array, pltpu.VMEM)


def shards(
    tokens, gain_attn, qkv_fine, scale_fine, out_fine, gain_ffn, ffn_in, ffn_out,
    up_proj, gain_coarse, qkv_coarse, scale_coarse, out_coarse,
):
    rows, cols, width = tokens.shape
    count = rows * cols
    strip = RADIUS * cols
    side = rounded_up((rows + 2 * RADIUS) * RADIUS, 16)
    heads = width // HD
    width_c = out_coarse.shape[0]
    heads_c = width_c // HD
    devices = lax.axis_size("ha") * lax.axis_size("wa")
    axes = ("ha", "wa")

    def shifted(array, axis, forward):
        size = lax.axis_size(axis)
        pairs = [(i, i + 1) if forward else (i + 1, i) for i in range(size - 1)]
        return lax.ppermute(array, axis, pairs)

    flat = tokens.reshape(count, width)
    up = shifted(flat[count - strip :], "ha", True)
    down = shifted(flat[:strip], "ha", False)
    left_edge, right_edge = pl.pallas_call(
        functools.partial(edge_kernel, rows, cols),
        out_shape=[jax.ShapeDtypeStruct((side, width), BF)] * 2,
        in_specs=[vmem()] * 3,
        out_specs=[vmem()] * 2,
        name="edges",
    )(flat, up, down)
    left = shifted(right_edge, "wa", True)
    right = shifted(left_edge, "wa", False)

    fine, pooled = pl.pallas_call(
        functools.partial(fine_kernel, rows, cols, heads, axes),
        out_shape=[
            jax.ShapeDtypeStruct((count, width), BF),
            jax.ShapeDtypeStruct((1, width), BF),
        ],
        in_specs=[vmem()] * 7 + [smem()] + [vmem()] * 4,
        out_specs=[vmem()] * 2,
        compiler_params=pltpu.CompilerParams(vmem_limit_bytes=24 * MIB),
        name="fine",
    )(
        flat, up, down, left, right, gain_attn.reshape(1, -1), in_vmem(qkv_fine), scale_fine,
        in_vmem(out_fine), gain_ffn.reshape(1, -1), in_vmem(ffn_in), in_vmem(ffn_out),
    )

    every = lax.all_gather(pooled, axes, axis=0, tiled=True)
    coarse_out = pl.pallas_call(
        functools.partial(coarse_kernel, heads_c, axes),
        out_shape=jax.ShapeDtypeStruct((1, width_c), BF),
        in_specs=[vmem()] * 4 + [smem()] + [vmem()],
        out_specs=vmem(),
        scratch_shapes=[pltpu.VMEM((devices, width_c), F32)] * 2,
        compiler_params=pltpu.CompilerParams(vmem_limit_bytes=24 * MIB),
        name="coarse",
    )(
        every, in_vmem(up_proj), gain_coarse.reshape(1, -1), in_vmem(qkv_coarse), scale_coarse,
        in_vmem(out_coarse),
    )
    return fine.reshape(rows, cols, width), coarse_out.reshape(1, 1, width_c)


def solution(mesh):
    return jax.shard_map(
        shards,
        mesh=mesh,
        in_specs=(P("ha", "wa", None), P(), P(), P(), P(), P(), P(), P(), P(), P(), P(), P(), P()),
        out_specs=(P("ha", "wa", None), P("ha", "wa", None)),
        check_vma=False,
    )
```

time: 486 us -> 112 us (0.23)
  the two profiles are of different devices: /device:TPU:0 before, /device:TPU:4 now
where the time goes in v1:
time: 112 us; the launch traced here: 111 us
  blocking collectives  66.2 us (59%)
  local copies, waits for them, and re-layouts  16.5 us (15%)
  starting transfers between devices  11.2 us (10%)
  Pallas kernels  10.5 us (9%)
  waiting for transfers between devices  6.29 us (6%)
    all_gather x1, blocking collectives, shards(): every = lax.all_gather(pooled, axes, axis=0, tiled=True)  66.2 us
    unnamed x35, local copies, waits for them, and re-layouts  15.8 us
    ppermute x4, starting transfers between devices, shifted(): return lax.ppermute(array, axis, pairs)  11.2 us
    ppermute x4, waiting for transfers between devices, shifted(): return lax.ppermute(array, axis, pairs)  6.29 us
    pallas_call x1, Pallas kernels, shards(): pl.pallas_call(functools.partial(coarse_kernel, heads_c, axes), out_shape...  4.72 us
    pallas_call x1, Pallas kernels, shards(): pl.pallas_call(functools.partial(fine_kernel, rows, cols, heads, axes), o...  4.06 us
  transfers between devices with their start and end apart: 4, of which 3 were waited for; matrix products, arithmetic and copies ran while one was open for 0% of the time, Pallas kernels for 0%

profile of v1, /device:TPU:4, one launch (start us, length us, event | category | flops | bytes accessed | tf_op | source)
XLA Modules:
  0.0 111.5 jit_solution(5087559970082969242)
XLA Ops:
  0.6 0.8 fusion
  1.4 1.9 %collective-permute-start = (bf16[48,256]{1,0:T(8,128)(2,1)S(1)}, bf16[48,256]{1,0:T(8,128)(2,1)S(1)}, u32[]{:S(2)}, u32[]{:S(2)}) collective-permute-start(bf16[48,256]{1,0:T(8,128)(2,1)S(1)} %bitcast.20), channel_id=1, source_target_pairs={{0,4},{4,8},{8,12},{12,16},{16,20},{20,24},{24,28},{1,5},{5,9},{9,... | collective-permute-start | bytes 73736 | tf_op jit(solution)/shard_map/ppermute | solution.py:237
  3.3 4.5 %collective-permute-start.1 = (bf16[48,256]{1,0:T(8,128)(2,1)S(1)}, bf16[48,256]{1,0:T(8,128)(2,1)S(1)}, u32[]{:S(2)}, u32[]{:S(2)}) collective-permute-start(bf16[48,256]{1,0:T(8,128)(2,1)S(1)} %bitcast.19), channel_id=1, source_target_pairs={{4,0},{8,4},{12,8},{16,12},{20,16},{24,20},{28,24},{5,1},{9,5},{13... | collective-permute-start | bytes 73736 | tf_op jit(solution)/shard_map/ppermute | solution.py:237
  7.9 0.0 collective-permute-done.up_ref
  7.9 0.0 copy-start.8
  7.9 1.5 %collective-permute-done.1.down_ref = bf16[48,256]{1,0:T(8,128)(2,1)S(1)} collective-permute-done((bf16[48,256]{1,0:T(8,128)(2,1)S(1)}, bf16[48,256]{1,0:T(8,128)(2,1)S(1)}, u32[]{:S(2)}, u32[]{:S(2)}) %collective-permute-start.1) | collective-permute-done | bytes 24608 | tf_op jit(solution)/shard_map/ppermute | solution.py:237
  9.4 0.0 copy-start.10
  9.4 0.0 copy-done.8
  9.4 0.6 copy-done.10
  10.0 1.8 %edges.1 = (bf16[80,256]{1,0:T(8,128)(2,1)}, bf16[80,256]{1,0:T(8,128)(2,1)}) custom-call(bf16[256,256]{1,0:T(8,128)(2,1)} %bitcast.12, bf16[48,256]{1,0:T(8,128)(2,1)} %copy-done.8, bf16[48,256]{1,0:T(8,128)(2,1)} %copy-done.10), custom_call_target="tpu_custom_call" | custom-call | tf_op jit(solution)/shard_map/edges/pallas_call | solution.py:242
  11.7 3.5 %collective-permute-start.2 = (bf16[80,256]{1,0:T(8,128)(2,1)}, bf16[80,256]{1,0:T(8,128)(2,1)S(1)}, u32[]{:S(2)}, u32[]{:S(2)}) collective-permute-start(bf16[80,256]{1,0:T(8,128)(2,1)} %get-tuple-element.6), channel_id=1, source_target_pairs={{0,1},{1,2},{2,3},{4,5},{5,6},{6,7},{8,9},{9,10},{10,11},{12,13},{... | collective-permute-start | bytes 122888 | tf_op jit(solution)/shard_map/ppermute | solution.py:237
  15.2 1.3 %collective-permute-start.3 = (bf16[80,256]{1,0:T(8,128)(2,1)}, bf16[80,256]{1,0:T(8,128)(2,1)S(1)}, u32[]{:S(2)}, u32[]{:S(2)}) collective-permute-start(bf16[80,256]{1,0:T(8,128)(2,1)} %get-tuple-element.7), channel_id=1, source_target_pairs={{1,0},{2,1},{3,2},{5,4},{6,5},{7,6},{9,8},{10,9},{11,10},{13,12},{... | collective-permute-start | bytes 122888 | tf_op jit(solution)/shard_map/ppermute | solution.py:237
  16.5 0.7 collective-permute-done.2.left_ref
  17.2 4.1 %collective-permute-done.3.right_ref = bf16[80,256]{1,0:T(8,128)(2,1)S(1)} collective-permute-done((bf16[80,256]{1,0:T(8,128)(2,1)}, bf16[80,256]{1,0:T(8,128)(2,1)S(1)}, u32[]{:S(2)}, u32[]{:S(2)}) %collective-permute-start.3) | collective-permute-done | bytes 40992 | tf_op jit(solution)/shard_map/ppermute | solution.py:237
  21.3 0.0 copy-start.2
  21.3 1.1 %copy-done.2 = bf16[256,1536]{1,0:T(8,128)(2,1)S(1)} copy-done((bf16[256,1536]{1,0:T(8,128)(2,1)S(1)}, bf16[256,1536]{1,0:T(8,128)(2,1)}, u32[]{:S(2)}) %copy-start.2) | copy-done | bytes 786456
  22.4 0.0 copy-start.3
  22.4 0.9 copy-done.3
  23.3 0.0 copy-start.5
  23.3 1.0 copy-done.5
  24.3 0.0 copy-start.6
  24.3 1.0 copy-done.6
  25.3 0.0 copy-start.7
  25.3 0.9 copy-done.7
  26.2 0.0 copy-start.9
  26.2 0.7 copy-done.9
  27.0 0.0 copy-start.11
  27.0 0.7 copy-done.11
  27.7 0.0 copy-start.13
  27.7 0.7 copy-done.13
  28.4 0.0 copy-start.14
  28.4 0.7 copy-done.14
  29.1 0.0 copy-start.15
  29.1 0.7 copy-done.15
  29.7 4.1 %fine.1 = (bf16[256,256]{1,0:T(8,128)(2,1)}, bf16[1,256]{1,0:T(2,128)(2,1)S(1)}) custom-call(bf16[256,256]{1,0:T(8,128)(2,1)S(1)} %bitcast.13, bf16[48,256]{1,0:T(8,128)(2,1)S(1)} %copy-done.9, bf16[48,256]{1,0:T(8,128)(2,1)S(1)} %copy-done.11, bf16[80,256]{1,0:T(8,128)(2,1)S(1)} %collective-permute-done.2.left_ref, ...), custom_call_target="tpu_custom_call" | custom-call | tf_op jit(solution)/shard_map/fine/pallas_call | solution.py:252
  33.8 66.2 %all-gather = bf16[32,1,256]{2,1,0:T(2,128)(2,1)S(1)} all-gather(bf16[1,1,256]{2,1,0:T(2,128)(2,1)S(1)} %bitcast.18), channel_id=1, replica_groups=mesh['ha'=8,'wa'=4] {'ha','wa'}, dimensions={0}, use_global_device_ids=true | all-gather | bytes 16896 | tf_op jit(solution)/shard_map/all_gather | solution.py:267
  100.0 0.0 copy-start
  100.0 2.8 %copy-done = bf16[1024,3072]{1,0:T(8,128)(2,1)S(1)} copy-done((bf16[1024,3072]{1,0:T(8,128)(2,1)S(1)}, bf16[1024,3072]{1,0:T(8,128)(2,1)}, u32[]{:S(2)}) %copy-start) | copy-done | bytes 6291480
  102.8 0.0 copy-start.1
  102.8 1.6 %copy-done.1 = bf16[1024,1024]{1,0:T(8,128)(2,1)S(1)} copy-done((bf16[1024,1024]{1,0:T(8,128)(2,1)S(1)}, bf16[1024,1024]{1,0:T(8,128)(2,1)}, u32[]{:S(2)}) %copy-start.1) | copy-done | bytes 2097176
  104.4 0.0 copy-start.4
  104.4 1.0 copy-done.4
  105.4 0.0 copy-start.12
  105.4 0.7 copy-done.12
  106.1 0.0 copy-start.16
  106.1 0.7 copy-done.16
  106.7 4.7 %coarse.1 = bf16[1,1024]{1,0:T(2,128)(2,1)} custom-call(bf16[32,256]{1,0:T(8,128)(2,1)S(1)} %bitcast.14, bf16[256,1024]{1,0:T(8,128)(2,1)S(1)} %copy-done.4, f32[1,1024]{1,0:T(1,128)S(1)} %bitcast.15, bf16[1024,3072]{1,0:T(8,128)(2,1)S(1)} %copy-done, f32[16]{0:T(128)S(1)} %copy-done.16, bf16[1024,1024]{1,0:T(8,128)(2,1)S(1)} %copy-done.1), custom_call_target="tpu_custom_call" | custom-call | tf_op jit(solution)/shard_map/coarse/pallas_call | solution.py:268
  (1 shorter events, 0.0 us)
Async XLA Ops:
  1.4 6.5 %collective-permute-start = (bf16[48,256]{1,0:T(8,128)(2,1)S(1)}, bf16[48,256]{1,0:T(8,128)(2,1)S(1)}, u32[]{:S(2)}, u32[]{:S(2)}) collective-permute-start(bf16[48,256]{1,0:T(8,128)(2,1)S(1)} %bitcast.20), channel_id=1, source_target_pairs={{0,4},{4,8},{8,12},{12,16},{16,20},{20,24},{24,28},{1,5},{5,9},{9,... | collective-permute-start | bytes 73736 | tf_op jit(solution)/shard_map/ppermute | solution.py:237
  3.3 6.0 %collective-permute-start.1 = (bf16[48,256]{1,0:T(8,128)(2,1)S(1)}, bf16[48,256]{1,0:T(8,128)(2,1)S(1)}, u32[]{:S(2)}, u32[]{:S(2)}) collective-permute-start(bf16[48,256]{1,0:T(8,128)(2,1)S(1)} %bitcast.19), channel_id=1, source_target_pairs={{4,0},{8,4},{12,8},{16,12},{20,16},{24,20},{28,24},{5,1},{9,5},{13... | collective-permute-start | bytes 73736 | tf_op jit(solution)/shard_map/ppermute | solution.py:237
  7.9 1.5 %copy-start.8 = (bf16[48,256]{1,0:T(8,128)(2,1)}, bf16[48,256]{1,0:T(8,128)(2,1)S(1)}, u32[]{:S(2)}) copy-start(bf16[48,256]{1,0:T(8,128)(2,1)S(1)} %collective-permute-done.up_ref) | copy-start | bytes 73732
  9.4 0.6 copy-start.10
  11.7 5.5 %collective-permute-start.2 = (bf16[80,256]{1,0:T(8,128)(2,1)}, bf16[80,256]{1,0:T(8,128)(2,1)S(1)}, u32[]{:S(2)}, u32[]{:S(2)}) collective-permute-start(bf16[80,256]{1,0:T(8,128)(2,1)} %get-tuple-element.6), channel_id=1, source_target_pairs={{0,1},{1,2},{2,3},{4,5},{5,6},{6,7},{8,9},{9,10},{10,11},{12,13},{... | collective-permute-start | bytes 122888 | tf_op jit(solution)/shard_map/ppermute | solution.py:237
  15.2 6.1 %collective-permute-start.3 = (bf16[80,256]{1,0:T(8,128)(2,1)}, bf16[80,256]{1,0:T(8,128)(2,1)S(1)}, u32[]{:S(2)}, u32[]{:S(2)}) collective-permute-start(bf16[80,256]{1,0:T(8,128)(2,1)} %get-tuple-element.7), channel_id=1, source_target_pairs={{1,0},{2,1},{3,2},{5,4},{6,5},{7,6},{9,8},{10,9},{11,10},{13,12},{... | collective-permute-start | bytes 122888 | tf_op jit(solution)/shard_map/ppermute | solution.py:237
  21.3 1.1 %copy-start.2 = (bf16[256,1536]{1,0:T(8,128)(2,1)S(1)}, bf16[256,1536]{1,0:T(8,128)(2,1)}, u32[]{:S(2)}) copy-start(bf16[256,1536]{1,0:T(8,128)(2,1)} %ffn_in_ref.1) | copy-start | bytes 2359300
  22.4 0.9 copy-start.3
  23.3 1.0 copy-start.5
  24.3 1.0 copy-start.6
  25.3 0.9 copy-start.7
  26.2 0.7 copy-start.9
  27.0 0.7 copy-start.11
  27.7 0.7 copy-start.13
  28.4 0.7 copy-start.14
  29.1 0.7 copy-start.15
  100.0 2.8 %copy-start = (bf16[1024,3072]{1,0:T(8,128)(2,1)S(1)}, bf16[1024,3072]{1,0:T(8,128)(2,1)}, u32[]{:S(2)}) copy-start(bf16[1024,3072]{1,0:T(8,128)(2,1)} %qkv_ref.3) | copy-start | bytes 18874372
  102.8 1.6 %copy-start.1 = (bf16[1024,1024]{1,0:T(8,128)(2,1)S(1)}, bf16[1024,1024]{1,0:T(8,128)(2,1)}, u32[]{:S(2)}) copy-start(bf16[1024,1024]{1,0:T(8,128)(2,1)} %out_ref.3) | copy-start | bytes 6291460
  104.4 1.0 copy-start.4
  105.4 0.7 copy-start.12
  106.1 0.7 copy-start.16
